TPU v7x, 1024 devices: a whole 4x8x16 slice. The times are simulated.
1024 devices in a mesh: expert: 16 (over z), dp: 64 (over y, x, core).
Axes of the slice: x: 4, y: 8, z: 16, core: 2. Of those that a mesh axis runs over, the one named last changes fastest.
Arguments:
- tokens: bfloat16 [2560, 4096], P('dp', 'expert'), may hold values from -6 to 6
- expert_ids: int32 [2560, 8], P('dp'), may hold values from 0 to 63, all different within a row; in each aligned block of 40 rows (0 to 39, 40 to 79, ...) at most 7 rows name the same one
- gate_probs: float32 [2560, 8], P('dp'), may hold values from 0.1 to 1
- cotangent: bfloat16 [2560, 4096], P('dp', 'expert'), may hold values from -6 to 6
- w_gate: bfloat16 [64, 1024, 4096], P('dp', None, 'expert'), may hold values from -0.09375 to 0.09375
- w_up: bfloat16 [64, 1024, 4096], P('dp', None, 'expert'), may hold values from -0.09375 to 0.09375
- w_down: bfloat16 [64, 1024, 4096], P('dp', None, 'expert'), may hold values from -0.1875 to 0.1875
Outputs:
- mixed: bfloat16 [2560, 4096], P('dp', 'expert')
- token_grad: bfloat16 [2560, 4096], P('dp', 'expert')
- gate_grad: bfloat16 [64, 1024, 4096], P('dp', None, 'expert')
- up_grad: bfloat16 [64, 1024, 4096], P('dp', None, 'expert')
- down_grad: bfloat16 [64, 1024, 4096], P('dp', None, 'expert')
Inputs may be any that keep to these rules, and one draw needn't show every extreme that they name: `expert_ids`: each token names 8 different experts. Among the 40 tokens of one index of dp at most 7 name any one expert, and in some such block one expert is named by exactly 7 of them.
All inputs are finite; a program needn't handle non-finite values.
Results may differ from a plain program's by a relative error of at most 0.03.
Values may be sent and summed in bfloat16 or wider, within the bound.
A program may use at most 32 MiB of HBM per device.

v0:
```python
import jax
import jax.numpy as jnp
from jax import lax
from jax.sharding import PartitionSpec as P


def slot_places(expert_ids, experts, capacity):
    onehot = (expert_ids[:, :, None] == jnp.arange(experts, dtype=jnp.int32)[None, None, :]).astype(
        jnp.int32
    )
    per_token = jnp.sum(onehot, axis=1)
    earlier = jnp.cumsum(per_token, axis=0) - per_token
    slot = jnp.sum(onehot * earlier[:, None, :], axis=2)
    flat = expert_ids * capacity + slot
    return (
        flat[:, :, None] == jnp.arange(experts * capacity, dtype=jnp.int32)[None, None, :]
    ).astype(jnp.float32)


def gate_deltas(gate_pre, up_pre, hidden_grad):
    sigmoid_gate = jax.nn.sigmoid(gate_pre)
    active = gate_pre * sigmoid_gate
    gate_delta = (
        hidden_grad * up_pre * sigmoid_gate * (1.0 + gate_pre * (1.0 - sigmoid_gate))
    ).astype(jnp.bfloat16)
    up_delta = (hidden_grad * active).astype(jnp.bfloat16)
    return (gate_delta, up_delta)


def shards(tokens, expert_ids, gate_probs, cotangent, w_gate, w_up, w_down):
    experts = lax.axis_size("dp")
    tok_count = tokens.shape[0]
    top_count = expert_ids.shape[1]
    capacity = min(tok_count, max(2, 3 * tok_count * top_count // (2 * experts)))
    slices = tokens.shape[1]
    places = slot_places(expert_ids, experts, capacity)
    select = jnp.sum(places, axis=1)
    weighted = jnp.sum(places * gate_probs[:, :, None], axis=1)
    xbuf = jnp.einsum(
        "tc,td->cd", select.astype(jnp.bfloat16), tokens, preferred_element_type=jnp.float32
    ).astype(jnp.bfloat16)
    scaled = (gate_probs[:, :, None] * cotangent[:, None, :].astype(jnp.float32)).astype(
        jnp.bfloat16
    )
    dbuf = jnp.einsum(
        "tkc,tkd->cd", places.astype(jnp.bfloat16), scaled, preferred_element_type=jnp.float32
    ).astype(jnp.bfloat16)
    x_in, d_in = (
        lax.all_to_all(
            xbuf.reshape(experts, capacity, slices), "dp", split_axis=0, concat_axis=0, tiled=True
        ),
        lax.all_to_all(
            dbuf.reshape(experts, capacity, slices), "dp", split_axis=0, concat_axis=0, tiled=True
        ),
    )
    row_count = x_in.shape[0] * capacity
    full_x = x_in.reshape(row_count, slices)
    full_d = d_in.reshape(row_count, slices)
    gate_w = w_gate[0]
    up_w = w_up[0]
    down_w = w_down[0]
    across = (((1,), (1,)), ((), ()))
    down_rows = (((0,), (0,)), ((), ()))
    gate_part = lax.dot_general(full_x, gate_w, across, preferred_element_type=jnp.float32)
    up_part = lax.dot_general(full_x, up_w, across, preferred_element_type=jnp.float32)
    grad_part = lax.dot_general(full_d, down_w, across, preferred_element_type=jnp.float32)
    gate_share, up_share, grad_share = (
        lax.psum_scatter(
            gate_part.astype(jnp.bfloat16), "expert", scatter_dimension=0, tiled=True
        ).astype(jnp.float32),
        lax.psum_scatter(
            up_part.astype(jnp.bfloat16), "expert", scatter_dimension=0, tiled=True
        ).astype(jnp.float32),
        lax.psum_scatter(
            grad_part.astype(jnp.bfloat16), "expert", scatter_dimension=0, tiled=True
        ).astype(jnp.float32),
    )
    hidden_share = (jax.nn.silu(gate_share) * up_share).astype(jnp.bfloat16)
    gate_dshare, up_dshare = gate_deltas(gate_share, up_share, grad_share)
    hidden, gate_delta, up_delta = (
        lax.all_gather(hidden_share, "expert", axis=0, tiled=True),
        lax.all_gather(gate_dshare, "expert", axis=0, tiled=True),
        lax.all_gather(up_dshare, "expert", axis=0, tiled=True),
    )
    out_rows = jnp.dot(hidden, down_w, preferred_element_type=jnp.float32).astype(jnp.bfloat16)
    back_rows = (
        jnp.dot(gate_delta, gate_w, preferred_element_type=jnp.float32)
        + jnp.dot(up_delta, up_w, preferred_element_type=jnp.float32)
    ).astype(jnp.bfloat16)
    down_grad = lax.dot_general(
        hidden, full_d, down_rows, preferred_element_type=jnp.float32
    ).astype(jnp.bfloat16)
    gate_grad = lax.dot_general(
        gate_delta, full_x, down_rows, preferred_element_type=jnp.float32
    ).astype(jnp.bfloat16)
    up_grad = lax.dot_general(
        up_delta, full_x, down_rows, preferred_element_type=jnp.float32
    ).astype(jnp.bfloat16)
    out_back, grad_back = (
        lax.all_to_all(
            out_rows.reshape(experts, capacity, slices),
            "dp",
            split_axis=0,
            concat_axis=0,
            tiled=True,
        ),
        lax.all_to_all(
            back_rows.reshape(experts, capacity, slices),
            "dp",
            split_axis=0,
            concat_axis=0,
            tiled=True,
        ),
    )
    mixed = jnp.dot(
        weighted,
        out_back.reshape(experts * capacity, slices).astype(jnp.float32),
        precision=lax.Precision.HIGHEST,
        preferred_element_type=jnp.float32,
    ).astype(jnp.bfloat16)
    token_grad = jnp.dot(
        select,
        grad_back.reshape(experts * capacity, slices).astype(jnp.float32),
        precision=lax.Precision.HIGHEST,
        preferred_element_type=jnp.float32,
    ).astype(jnp.bfloat16)
    return (mixed, token_grad, gate_grad[None], up_grad[None], down_grad[None])


def solution(mesh):
    in_specs = (
        P("dp", "expert"),
        P("dp", None),
        P("dp", None),
        P("dp", "expert"),
        P("dp", None, "expert"),
        P("dp", None, "expert"),
        P("dp", None, "expert"),
    )
    out_specs = (
        P("dp", "expert"),
        P("dp", "expert"),
        P("dp", None, "expert"),
        P("dp", None, "expert"),
        P("dp", None, "expert"),
    )
    return jax.shard_map(shards, mesh=mesh, in_specs=in_specs, out_specs=out_specs, check_vma=False)
```

profile of v0, /device:TPU:1, one launch (start us, length us, event | category | flops | bytes accessed | tf_op | source)
XLA Modules:
  0.0 272.8 jit_solution(9644377351909715591)
XLA Ops:
  0.7 0.8 copy.18
  1.7 0.8 select_reduce_fusion.1
  2.6 0.7 multiply_add_fusion
  3.3 1.5 convert_reduce_fusion
  4.8 0.6 copy-done.7
  5.4 1.0 convolution_convert_fusion.6
  6.4 0.8 reshape.48
  7.2 18.2 %all-to-all-start = ((bf16[64,7,256]{2,1,0:T(8,128)(2,1)}), bf16[64,7,256]{2,1,0:T(8,128)(2,1)S(1)}, u32[]{:S(2)}, u32[]{:S(2)}) async-start(bf16[64,7,256]{2,1,0:T(8,128)(2,1)} %reshape.48), calls=%async_computation | async-start | bytes 524288 | tf_op jit(solution)/shard_map/all_to_all | solution.py:49
  25.4 0.4 fusion.6
  25.9 0.8 reshape.52
  26.7 12.0 %all-to-all-done = bf16[64,7,256]{2,1,0:T(8,128)(2,1)S(1)} async-done(((bf16[64,7,256]{2,1,0:T(8,128)(2,1)}), bf16[64,7,256]{2,1,0:T(8,128)(2,1)S(1)}, u32[]{:S(2)}, u32[]{:S(2)}) %all-to-all-start) | async-done | bytes 229408 | tf_op jit(solution)/shard_map/all_to_all | solution.py:49
  38.7 4.7 %all-to-all-start.2 = ((bf16[64,7,256]{2,1,0:T(8,128)(2,1)}), bf16[64,7,256]{2,1,0:T(8,128)(2,1)S(1)}, u32[]{:S(2)}, u32[]{:S(2)}) async-start(bf16[64,7,256]{2,1,0:T(8,128)(2,1)} %reshape.52), calls=%async_computation.2 | async-start | bytes 524288 | tf_op jit(solution)/shard_map/all_to_all | solution.py:52
  43.5 0.4 convolution_convert_fusion.1
  44.0 0.4 convolution_convert_fusion.2
  44.4 12.1 %all-to-all-done.2 = bf16[64,7,256]{2,1,0:T(8,128)(2,1)S(1)} async-done(((bf16[64,7,256]{2,1,0:T(8,128)(2,1)}), bf16[64,7,256]{2,1,0:T(8,128)(2,1)S(1)}, u32[]{:S(2)}, u32[]{:S(2)}) %all-to-all-start.2) | async-done | bytes 229408 | tf_op jit(solution)/shard_map/all_to_all | solution.py:52
  56.7 1.6 convolution_convert_fusion
  58.2 46.0 %fusion.31 = (bf16[32,1024]{1,0:T(8,128)(2,1)}, bf16[32,1024]{1,0:T(8,128)(2,1)}, bf16[32,1024]{1,0:T(8,128)(2,1)}) fusion(bf16[448,1024]{1,0:T(8,128)(2,1)S(1)} %convolution_convert_fusion.1, bf16[448,1024]{1,0:T(8,128)(2,1)S(1)} %convolution_convert_fusion.2, bf16[448,1024]{1,0:T(8,128)(2,1)S(1)} %convolution_convert_fusion), kind=kCustom, calls=%all-reduce-scatter.3 | all-reduce-scatter fusion | flops 1572865 | bytes 2953216
  104.2 0.9 slice.1
  105.1 1.8 collective-permute-start.3
  106.9 2.3 collective-permute-start.2
  109.2 2.6 collective-permute-start
  111.8 2.2 collective-permute-start.4
  114.0 0.9 slice
  114.9 1.9 collective-permute-start.1
  116.8 0.9 slice.2
  117.7 4.0 %collective-permute-start.5 = (bf16[28,1024]{1,0:T(8,128)(2,1)S(1)}, bf16[28,1024]{1,0:T(8,128)(2,1)S(1)}, u32[]{:S(2)}, u32[]{:S(2)}) collective-permute-start(bf16[28,1024]{1,0:T(8,128)(2,1)S(1)} %slice.2), channel_id=1, source_target_pairs={{0,128},{64,192},{128,256},{192,320},{256,384},{320,448},{384,512}... | collective-permute-start | bytes 172040
  121.7 1.3 dynamic-slice.8
  123.7 1.1 concatenate.1
  124.8 1.1 concatenate
  125.9 0.4 concatenate.2
  126.5 28.1 %all-gather.1 = bf16[16,28,1024]{2,1,0:T(8,128)(2,1)S(1)} all-gather(bf16[1,28,1024]{2,1,0:T(8,128)(2,1)S(1)} %get-tuple-element.14), channel_id=1, replica_groups=mesh['expert'=16,'dp'=64] {'expert'}, dimensions={0}, use_global_device_ids=true | all-gather | bytes 974848 | tf_op jit(solution)/shard_map/all_gather | solution.py:82
  154.8 1.2 fusion.12
  156.0 26.4 %all-gather.2 = bf16[16,28,1024]{2,1,0:T(8,128)(2,1)S(1)} all-gather(bf16[1,28,1024]{2,1,0:T(8,128)(2,1)S(1)} %get-tuple-element.13), channel_id=1, replica_groups=mesh['expert'=16,'dp'=64] {'expert'}, dimensions={0}, use_global_device_ids=true | all-gather | bytes 974848 | tf_op jit(solution)/shard_map/all_gather | solution.py:83
  182.5 1.6 fusion.7
  184.1 0.8 reshape.54
  184.9 24.2 %all-to-all-start.3 = ((bf16[64,7,256]{2,1,0:T(8,128)(2,1)}), bf16[64,7,256]{2,1,0:T(8,128)(2,1)}, u32[]{:S(2)}, u32[]{:S(2)}) async-start(bf16[64,7,256]{2,1,0:T(8,128)(2,1)} %reshape.54), calls=%async_computation.3 | async-start | bytes 524288 | tf_op jit(solution)/shard_map/all_to_all | solution.py:107
  209.1 28.7 %all-gather = bf16[16,28,1024]{2,1,0:T(8,128)(2,1)S(1)} all-gather(bf16[1,28,1024]{2,1,0:T(8,128)(2,1)S(1)} %get-tuple-element.15), channel_id=1, replica_groups=mesh['expert'=16,'dp'=64] {'expert'}, dimensions={0}, use_global_device_ids=true | all-gather | bytes 974848 | tf_op jit(solution)/shard_map/all_gather | solution.py:81
  237.8 1.1 reshape.57
  238.9 1.8 convolution_convert_fusion.7
  240.6 0.8 reshape.50
  241.4 1.3 fusion.3
  242.8 15.9 %all-to-all-start.1 = ((bf16[64,7,256]{2,1,0:T(8,128)(2,1)}), bf16[64,7,256]{2,1,0:T(8,128)(2,1)S(1)}, u32[]{:S(2)}, u32[]{:S(2)}) async-start(bf16[64,7,256]{2,1,0:T(8,128)(2,1)} %reshape.50), calls=%async_computation.1 | async-start | bytes 524288 | tf_op jit(solution)/shard_map/all_to_all | solution.py:100
  258.7 1.3 fusion.4
  260.0 1.3 fusion.5
  261.3 1.1 reshape.55
  262.4 0.8 convolution_convert_fusion.8
  263.2 8.6 %all-to-all-done.1 = bf16[64,7,256]{2,1,0:T(8,128)(2,1)S(1)} async-done(((bf16[64,7,256]{2,1,0:T(8,128)(2,1)}), bf16[64,7,256]{2,1,0:T(8,128)(2,1)S(1)}, u32[]{:S(2)}, u32[]{:S(2)}) %all-to-all-start.1) | async-done | bytes 229408 | tf_op jit(solution)/shard_map/all_to_all | solution.py:100
  271.9 0.8 convolution_convert_fusion.9
  (43 shorter events, 1.1 us)
Async XLA Ops:
  0.6 43.3 %copy-start = (bf16[1,1024,256]{2,1,0:T(8,128)(2,1)S(1)}, bf16[1,1024,256]{2,1,0:T(8,128)(2,1)}, u32[]{:S(2)}) copy-start(bf16[1,1024,256]{2,1,0:T(8,128)(2,1)} %param.11) | copy-start | bytes 1572868
  0.6 24.8 %copy-start.12 = (f32[40,8]{0,1:T(8,128)S(1)}, f32[40,8]{0,1:T(8,128)}, u32[]{:S(2)}) copy-start(f32[40,8]{0,1:T(8,128)} %param.9) | copy-start | bytes 3844
  0.7 24.8 %copy-start.11 = (bf16[40,256]{1,0:T(8,128)(2,1)S(1)}, bf16[40,256]{1,0:T(8,128)(2,1)}, u32[]{:S(2)}) copy-start(bf16[40,256]{1,0:T(8,128)(2,1)} %param.10) | copy-start | bytes 61444
  4.8 0.6 copy-start.7
  7.2 31.5 %all-to-all-start = ((bf16[64,7,256]{2,1,0:T(8,128)(2,1)}), bf16[64,7,256]{2,1,0:T(8,128)(2,1)S(1)}, u32[]{:S(2)}, u32[]{:S(2)}) async-start(bf16[64,7,256]{2,1,0:T(8,128)(2,1)} %reshape.48), calls=%async_computation | async-start | bytes 524288 | tf_op jit(solution)/shard_map/all_to_all | solution.py:49
  25.9 17.6 %copy-start.1 = (bf16[1,1024,256]{2,1,0:T(8,128)(2,1)S(1)}, bf16[1,1024,256]{2,1,0:T(8,128)(2,1)}, u32[]{:S(2)}) copy-start(bf16[1,1024,256]{2,1,0:T(8,128)(2,1)} %param.12) | copy-start | bytes 1572868
  38.7 17.9 %all-to-all-start.2 = ((bf16[64,7,256]{2,1,0:T(8,128)(2,1)}), bf16[64,7,256]{2,1,0:T(8,128)(2,1)S(1)}, u32[]{:S(2)}, u32[]{:S(2)}) async-start(bf16[64,7,256]{2,1,0:T(8,128)(2,1)} %reshape.52), calls=%async_computation.2 | async-start | bytes 524288 | tf_op jit(solution)/shard_map/all_to_all | solution.py:52
  43.5 0.9 copy-start.2
  56.7 47.5 %copy-start.4 = (bf16[448,256]{1,0:T(8,128)(2,1)}, bf16[448,256]{1,0:T(8,128)(2,1)S(1)}, u32[]{:S(2)}) copy-start(bf16[448,256]{1,0:T(8,128)(2,1)S(1)} %reshape.53) | copy-start | bytes 688132
  104.2 21.7 %copy-start.9 = (bf16[32,1024]{1,0:T(8,128)(2,1)S(1)}, bf16[32,1024]{1,0:T(8,128)(2,1)}, u32[]{:S(2)}) copy-start(bf16[32,1024]{1,0:T(8,128)(2,1)} %get-tuple-element.12) | copy-start | bytes 196612
  105.1 12.6 %collective-permute-start.3 = (bf16[28,1024]{1,0:T(8,128)(2,1)S(1)}, bf16[28,1024]{1,0:T(8,128)(2,1)S(1)}, u32[]{:S(2)}, u32[]{:S(2)}) collective-permute-start(bf16[28,1024]{1,0:T(8,128)(2,1)S(1)} %slice.1), channel_id=1, source_target_pairs={{0,128},{64,192},{128,256},{192,320},{256,384},{320,448},{384,512}... | collective-permute-start | bytes 172040
  106.9 16.7 %collective-permute-start.2 = (bf16[32,1024]{1,0:T(8,128)(2,1)}, bf16[32,1024]{1,0:T(8,128)(2,1)S(1)}, u32[]{:S(2)}, u32[]{:S(2)}) collective-permute-start(bf16[32,1024]{1,0:T(8,128)(2,1)} %get-tuple-element.10), channel_id=1, source_target_pairs={{0,64},{64,128},{128,192},{192,256},{256,320},{320,384},{384,448},... | collective-permute-start | bytes 196616
  109.2 15.6 %collective-permute-start = (bf16[32,1024]{1,0:T(8,128)(2,1)}, bf16[32,1024]{1,0:T(8,128)(2,1)S(1)}, u32[]{:S(2)}, u32[]{:S(2)}) collective-permute-start(bf16[32,1024]{1,0:T(8,128)(2,1)} %get-tuple-element.11), channel_id=1, source_target_pairs={{0,64},{64,128},{128,192},{192,256},{256,320},{320,384},{384,448},... | collective-permute-start | bytes 196616
  111.8 14.1 %collective-permute-start.4 = (bf16[32,1024]{1,0:T(8,128)(2,1)}, bf16[32,1024]{1,0:T(8,128)(2,1)S(1)}, u32[]{:S(2)}, u32[]{:S(2)}) collective-permute-start(bf16[32,1024]{1,0:T(8,128)(2,1)} %get-tuple-element.12), channel_id=1, source_target_pairs={{0,64},{64,128},{128,192},{192,256},{256,320},{320,384},{384,448},... | collective-permute-start | bytes 196616
  114.9 9.9 %collective-permute-start.1 = (bf16[28,1024]{1,0:T(8,128)(2,1)S(1)}, bf16[28,1024]{1,0:T(8,128)(2,1)S(1)}, u32[]{:S(2)}, u32[]{:S(2)}) collective-permute-start(bf16[28,1024]{1,0:T(8,128)(2,1)S(1)} %slice), channel_id=1, source_target_pairs={{0,128},{64,192},{128,256},{192,320},{256,384},{320,448},{384,512}... | collective-permute-start | bytes 172040
  117.7 8.2 %collective-permute-start.5 = (bf16[28,1024]{1,0:T(8,128)(2,1)S(1)}, bf16[28,1024]{1,0:T(8,128)(2,1)S(1)}, u32[]{:S(2)}, u32[]{:S(2)}) collective-permute-start(bf16[28,1024]{1,0:T(8,128)(2,1)S(1)} %slice.2), channel_id=1, source_target_pairs={{0,128},{64,192},{128,256},{192,320},{256,384},{320,448},{384,512}... | collective-permute-start | bytes 172040
  184.9 57.9 %all-to-all-start.3 = ((bf16[64,7,256]{2,1,0:T(8,128)(2,1)}), bf16[64,7,256]{2,1,0:T(8,128)(2,1)}, u32[]{:S(2)}, u32[]{:S(2)}) async-start(bf16[64,7,256]{2,1,0:T(8,128)(2,1)} %reshape.54), calls=%async_computation.3 | async-start | bytes 524288 | tf_op jit(solution)/shard_map/all_to_all | solution.py:107
  238.9 2.6 copy-start.3
  242.8 29.1 %all-to-all-start.1 = ((bf16[64,7,256]{2,1,0:T(8,128)(2,1)}), bf16[64,7,256]{2,1,0:T(8,128)(2,1)S(1)}, u32[]{:S(2)}, u32[]{:S(2)}) async-start(bf16[64,7,256]{2,1,0:T(8,128)(2,1)} %reshape.50), calls=%async_computation.1 | async-start | bytes 524288 | tf_op jit(solution)/shard_map/all_to_all | solution.py:100
  258.7 1.3 copy-start.5
  258.7 1.3 copy-start.6
  260.0 2.4 copy-start.8
  261.3 10.6 %copy-start.10 = (f32[40,448]{1,0:T(8,128)S(1)}, f32[40,448]{1,0:T(8,128)}, u32[]{:S(2)}) copy-start(f32[40,448]{1,0:T(8,128)} %get-tuple-element.6) | copy-start | bytes 215044
where the time goes:
time: 274 us; the launch traced here: 273 us
  blocking collectives  129 us (47%)
  starting transfers between devices  77.9 us (28%)
  waiting for transfers between devices  32.8 us (12%)
  local copies, waits for them, and re-layouts  14 us (5%)
  matrix products  13.9 us (5%)
  other arithmetic  3.35 us (1%)
    unnamed x1, blocking collectives  46 us
    all_gather x1, blocking collectives, shards(): lax.all_gather(hidden_share, 'expert', axis=0, tiled=True)  28.7 us
    all_gather x1, blocking collectives, shards(): lax.all_gather(gate_dshare, 'expert', axis=0, tiled=True)  28.1 us
    all_gather x1, blocking collectives, shards(): lax.all_gather(up_dshare, 'expert', axis=0, tiled=True)  26.4 us
    all_to_all x1, starting transfers between devices, shards(): lax.all_to_all(back_rows.reshape(experts, capacity, slices), 'dp', split_...  24.2 us
    all_to_all x1, starting transfers between devices, shards(): lax.all_to_all(xbuf.reshape(experts, capacity, slices), 'dp', split_axis=...  18.2 us
    all_to_all x1, starting transfers between devices, shards(): lax.all_to_all(out_rows.reshape(experts, capacity, slices), 'dp', split_a...  15.9 us
    unnamed x6, starting transfers between devices  14.9 us
  transfers between devices with their start and end apart: 10, of which 3 were waited for; matrix products, arithmetic and copies ran while one was open for 6% of the time, Pallas kernels for 0%

commit v1 on v0

v1 whole, which is shorter than its diff:
```python
import functools

import jax
import jax.numpy as jnp
from jax import lax
from jax.experimental import pallas as pl
from jax.experimental.pallas import tpu as pltpu
from jax.sharding import PartitionSpec as P

SLOTS = 8
PAIR = 2 * SLOTS
MESH = pl.DeviceIdType.MESH


def matmul(a, b, contract):
    return lax.dot_general(a, b, ((contract[0:1], contract[1:2]), ((), ())), preferred_element_type=jnp.float32)


def plan(n_z, n_dp):
    cores = 2 if n_dp >= 4 else 1
    width = 4 if n_dp >= 64 else 2
    height = n_dp // (cores * width)
    low = n_z // width
    return cores, width, height, low, n_dp // n_z


def kernel(
    n_z, n_dp, ids_ref, probs_ref, tok_ref, cot_ref, gate_hbm, up_hbm, down_hbm,
    mixed_ref, tgrad_ref, ggrad_hbm, ugrad_hbm, dgrad_hbm,
    wts, grads, route, sbuf, inbuf, obuf, rbuf, xall, dall, part, landed, held,
    w_sem, g_sem, in_send, in_recv, out_send, out_recv, rs_send, rs_recv, ag_send, ag_recv,
):
    cores, width, height, low, per = plan(n_z, n_dp)
    rows = per * SLOTS
    span = per * PAIR
    half, cut = n_z // 2, rows // 2
    n_tok, top = ids_ref.shape
    z = lax.axis_index("expert")
    g = lax.axis_index("dp")
    y, x, core = g // (width * cores), (g // cores) % width, g % cores
    z_right, z_left = (z + 1) % n_z, (z + n_z - 1) % n_z

    def partner(o, i, sign):
        dy = o // width + low * (i // cores)
        dx, dc = o % width, i % cores
        py = (y + sign * dy + height) % height
        px = (x + sign * dx + width) % width
        pc = (core + sign * dc + cores) % cores
        return (py * width + px) * cores + pc

    loads = [
        pltpu.make_async_copy(src.at[0], wts.at[n], w_sem.at[n])
        for n, src in enumerate((gate_hbm, up_hbm, down_hbm))
    ]
    for load in loads:
        load.start()

    barrier = pltpu.get_barrier_semaphore()

    @pl.loop(1, n_dp)
    def _(step):
        pl.semaphore_signal(barrier, inc=1, device_id={"dp": (g + step) % n_dp}, device_id_type=MESH)

    for near in (z_right, z_left):
        pl.semaphore_signal(barrier, inc=1, device_id={"expert": near}, device_id_type=MESH)

    lane = lax.broadcasted_iota(jnp.int32, (1, n_z * span), 1)
    o_of, i_of, r_of = lane // span, (lane % span) // PAIR, lane % PAIR
    ly = (y + o_of // width + low * (i_of // cores)) % height
    lx = (x + o_of % width) % width
    lc = (core + i_of % cores) % cores
    expert_of = (ly * width + lx) * cores + lc
    ids, probs = ids_ref[...], probs_ref[...]
    named = jnp.zeros((n_tok, n_z * span), jnp.float32)
    weight = jnp.zeros((n_tok, n_z * span), jnp.float32)
    for k in range(top):
        hit = ids[:, k : k + 1] == expert_of
        named = jnp.where(hit, 1.0, named)
        weight = jnp.where(hit, probs[:, k : k + 1], weight)
    before = (
        lax.broadcasted_iota(jnp.int32, (n_tok, n_tok), 1) < lax.broadcasted_iota(jnp.int32, (n_tok, n_tok), 0)
    ).astype(jnp.float32)
    slot = matmul(before, named, (1, 0))
    chosen = jnp.where(slot == (r_of % SLOTS).astype(jnp.float32), named, 0.0)
    first = r_of < SLOTS
    plain = jnp.where(first, chosen, 0.0)
    scale = jnp.where(first, 0.0, chosen * weight)
    high = scale.astype(jnp.bfloat16).astype(jnp.float32)
    mid = (scale - high).astype(jnp.bfloat16).astype(jnp.float32)
    route[...] = jnp.concatenate([plain, high, mid, scale - high - mid], axis=0).astype(jnp.bfloat16)
    tok, cot = tok_ref[...].astype(jnp.float32), cot_ref[...].astype(jnp.float32)
    values = jnp.concatenate([tok, cot, cot, cot], axis=0).astype(jnp.bfloat16)
    sbuf[...] = matmul(route[...], values, (0, 0)).astype(jnp.bfloat16)

    pl.semaphore_wait(barrier, n_dp + 1)

    def exchange(src, dst, send_sem, recv_sem, o, sign):
        for i in range(per):
            at = pl.ds(pl.multiple_of(o * span + i * PAIR, PAIR), PAIR)

            def remote():
                pltpu.make_async_remote_copy(
                    src_ref=src.at[at],
                    dst_ref=dst.at[at],
                    send_sem=send_sem,
                    recv_sem=recv_sem,
                    device_id={"dp": partner(o, i, sign)},
                    device_id_type=MESH,
                ).start()

            if i:
                remote()
            else:

                @pl.when(o == 0)
                def _():
                    pltpu.make_async_copy(src.at[at], dst.at[at], recv_sem).start()

                @pl.when(o != 0)
                def _():
                    remote()

    def wait_rows(ref, first_row, count, sem):
        view = ref.at[pl.ds(first_row, count)]
        pltpu.make_async_copy(view, view, sem).wait()

    def send_in(o):
        exchange(sbuf, inbuf, in_send, in_recv.at[o], o, 1)

    far = (z + half) % n_z
    send_in(far)

    @pl.loop(1, half)
    def _(s):
        send_in((z + half - s) % n_z)
        send_in((z + half + s) % n_z)

    send_in(z)
    for load in loads:
        load.wait()

    def partials(chunks):
        xs, ds = [], []
        for o in chunks:
            at = pl.multiple_of(o * span, span)
            wait_rows(inbuf, at, span, in_recv.at[o])
            both = inbuf[pl.ds(at, span), :].astype(jnp.float32).reshape(per, 2, SLOTS, -1)
            to = pl.ds(pl.multiple_of(o * rows, rows), rows)
            xs.append(both[:, 0].reshape(rows, -1).astype(jnp.bfloat16))
            ds.append(both[:, 1].reshape(rows, -1).astype(jnp.bfloat16))
            xall[to, :] = xs[-1]
            dall[to, :] = ds[-1]
        xrows = jnp.concatenate(xs, axis=0) if len(xs) > 1 else xs[0]
        drows = jnp.concatenate(ds, axis=0) if len(ds) > 1 else ds[0]
        for a, lhs in enumerate((xrows, xrows, drows)):
            product = matmul(lhs, wts[a], (1, 1)).astype(jnp.bfloat16)
            for n, o in enumerate(chunks):
                part[a, o] = product[n * rows : (n + 1) * rows]

    sides = (z_right, z_left)

    def rs_copy(d, s, a, o, at=None):
        src, dst = part.at[a, o], landed.at[d, s, a]
        if at is not None:
            src, dst = src.at[at], dst.at[at]
        return pltpu.make_async_remote_copy(
            src_ref=src,
            dst_ref=dst,
            send_sem=rs_send.at[d, s, a],
            recv_sem=rs_recv.at[d, s, a],
            device_id={"expert": sides[d]},
            device_id_type=MESH,
        )

    def ag_copy(d, s, a, o, at=None):
        src, dst = held.at[a, o], held.at[a, o]
        if at is not None:
            src, dst = src.at[at], dst.at[at]
        return pltpu.make_async_remote_copy(
            src_ref=src,
            dst_ref=dst,
            send_sem=ag_send.at[d, s, a],
            recv_sem=ag_recv.at[d, s, a],
            device_id={"expert": sides[d]},
            device_id_type=MESH,
        )

    halves = (pl.ds(0, cut), pl.ds(cut, cut))

    partials([far])
    for a in range(3):
        for d in range(2):
            rs_copy(d, 0, a, far, halves[d]).start()

    def ends(s):
        return (z + half - s) % n_z, (z + half + s) % n_z

    partials(ends(1))
    for a in range(3):
        for d in range(2):
            o = ends(1)[d]
            rs_copy(d, 0, a, o, halves[d]).wait_recv()
            at = halves[d]
            part[a, o, at, :] = (
                part[a, o, at, :].astype(jnp.float32) + landed[d, 0, a, at, :].astype(jnp.float32)
            ).astype(jnp.bfloat16)
            rs_copy(d, 1, a, o).start()

    @pl.loop(2, half)
    def _(s):
        chunks = ends(s)
        partials(chunks)
        for a in range(3):
            for d in range(2):
                o = chunks[d]
                rs_copy(d, s - 1, a, o).wait_recv()
                part[a, o] = (
                    part[a, o].astype(jnp.float32) + landed[d, s - 1, a].astype(jnp.float32)
                ).astype(jnp.bfloat16)
                rs_copy(d, s, a, o).start()

    partials([z])
    sums = []
    for a in range(3):
        for d in range(2):
            rs_copy(d, half - 1, a, z).wait_recv()
        sums.append(
            part[a, z].astype(jnp.float32)
            + landed[0, half - 1, a].astype(jnp.float32)
            + landed[1, half - 1, a].astype(jnp.float32)
        )
    gate, up, hgrad = sums
    sig = jax.nn.sigmoid(gate)
    active = gate * sig
    held[0, z] = (hgrad * up * sig * (1.0 + gate * (1.0 - sig))).astype(jnp.bfloat16)
    held[1, z] = (hgrad * active).astype(jnp.bfloat16)
    held[2, z] = (active * up).astype(jnp.bfloat16)
    for a in range(3):
        for d in range(2):
            ag_copy(d, 1, a, z).start()

    def outward(chunks):
        lhs = [
            jnp.concatenate([held[a, o] for o in chunks], axis=0) if len(chunks) > 1 else held[a, chunks[0]]
            for a in range(3)
        ]
        back = matmul(lhs[0], wts[0], (1, 0)) + matmul(lhs[1], wts[1], (1, 0))
        out = matmul(lhs[2], wts[2], (1, 0))
        for n, o in enumerate(chunks):
            mine = slice(n * rows, (n + 1) * rows)
            both = jnp.stack(
                [back[mine].reshape(per, SLOTS, -1), out[mine].reshape(per, SLOTS, -1)], axis=1
            ).reshape(span, -1)
            obuf[pl.ds(pl.multiple_of(o * span, span), span), :] = both.astype(jnp.bfloat16)
            exchange(obuf, rbuf, out_send, out_recv, o, -1)

    outward([z])

    @pl.loop(1, half - 1)
    def _(s):
        chunks = ((z - s + n_z) % n_z, (z + s) % n_z)
        for a in range(3):
            for d in range(2):
                ag_copy(d, s, a, chunks[d]).wait_recv()
                ag_copy(d, s + 1, a, chunks[d]).start()
        outward(chunks)

    last = ((z - (half - 1) + n_z) % n_z, (z + half - 1) % n_z)
    for a in range(3):
        for d in range(2):
            ag_copy(d, half - 1, a, last[d]).wait_recv()
            ag_copy(d, half, a, last[d], halves[d]).start()
    outward(last)
    for a in range(3):
        for d in range(2):
            ag_copy(d, half, a, far, halves[d]).wait_recv()
    outward([far])

    stores = []
    for a, dst in enumerate((ggrad_hbm, ugrad_hbm, dgrad_hbm)):
        whole = held[a].reshape(n_z * rows, -1)
        rhs = (dall if a == 2 else xall)[...]
        grads[a] = matmul(whole, rhs, (0, 0)).astype(jnp.bfloat16)
        stores.append(pltpu.make_async_copy(grads.at[a], dst.at[0], g_sem.at[a]))
        stores[-1].start()

    wait_rows(rbuf, 0, n_z * span, out_recv)
    total = matmul(route[...], rbuf[...], (1, 0))
    tgrad_ref[...] = total[:n_tok].astype(jnp.bfloat16)
    mixed_ref[...] = (total[n_tok : 2 * n_tok] + total[2 * n_tok : 3 * n_tok] + total[3 * n_tok :]).astype(
        jnp.bfloat16
    )

    wait_rows(sbuf, 0, n_z * span - PAIR, in_send)
    wait_rows(obuf, 0, n_z * span - PAIR, out_send)
    for a in range(3):
        for d in range(2):
            rs_copy(d, 0, a, far, halves[d]).wait_send()
            ag_copy(d, half, a, far, halves[d]).wait_send()

    @pl.loop(1, half)
    def _(s):
        for a in range(3):
            for d in range(2):
                rs_copy(d, s, a, z).wait_send()
                ag_copy(d, s, a, z).wait_send()

    for store in stores:
        store.wait()


def shards(n_z, n_dp, tokens, expert_ids, gate_probs, cotangent, w_gate, w_up, w_down):
    n_tok, feats = tokens.shape
    ff = w_gate.shape[1]
    rows = n_dp // n_z * SLOTS
    both = n_dp * PAIR
    half = n_z // 2
    bf16 = jnp.bfloat16
    vmem = pl.BlockSpec(memory_space=pltpu.VMEM)
    anywhere = pl.BlockSpec(memory_space=pl.ANY)
    act = jax.ShapeDtypeStruct((n_tok, feats), bf16)
    grad = jax.ShapeDtypeStruct((1, ff, feats), bf16)
    dma = pltpu.SemaphoreType.DMA
    return pl.pallas_call(
        functools.partial(kernel, n_z, n_dp),
        out_shape=(act, act, grad, grad, grad),
        in_specs=[vmem] * 4 + [anywhere] * 3,
        out_specs=(vmem, vmem, anywhere, anywhere, anywhere),
        scratch_shapes=[
            pltpu.VMEM((3, ff, feats), bf16),
            pltpu.VMEM((3, ff, feats), bf16),
            pltpu.VMEM((4 * n_tok, both), bf16),
            pltpu.VMEM((both, feats), bf16),
            pltpu.VMEM((both, feats), bf16),
            pltpu.VMEM((both, feats), bf16),
            pltpu.VMEM((both, feats), bf16),
            pltpu.VMEM((n_z * rows, feats), bf16),
            pltpu.VMEM((n_z * rows, feats), bf16),
            pltpu.VMEM((3, n_z, rows, ff), bf16),
            pltpu.VMEM((2, half, 3, rows, ff), bf16),
            pltpu.VMEM((3, n_z, rows, ff), bf16),
            dma((3,)),
            dma((3,)),
            dma,
            dma((n_z,)),
            dma,
            dma,
            dma((2, half, 3)),
            dma((2, half, 3)),
            dma((2, half + 1, 3)),
            dma((2, half + 1, 3)),
        ],
        compiler_params=pltpu.CompilerParams(
            collective_id=0, has_side_effects=True, vmem_limit_bytes=56 * 1024 * 1024
        ),
        name="experts",
    )(expert_ids, gate_probs, tokens, cotangent, w_gate, w_up, w_down)


def solution(mesh):
    n_z, n_dp = mesh.shape["expert"], mesh.shape["dp"]
    split = P("dp", "expert")
    weight = P("dp", None, "expert")
    return jax.shard_map(
        functools.partial(shards, n_z, n_dp),
        mesh=mesh,
        in_specs=(split, P("dp", None), P("dp", None), split, weight, weight, weight),
        out_specs=(split, split, weight, weight, weight),
        check_vma=False,
    )
```

time: 274 us -> 118 us (0.43)
  blocking collectives: 129 us -> 0 us
  Pallas kernels: 0 us -> 109 us
  starting transfers between devices: 77.9 us -> 0 us
  waiting for transfers between devices: 32.8 us -> 0 us
  matrix products: 13.9 us -> 0 us
  local copies, waits for them, and re-layouts: 14 us -> 7.96 us
  other arithmetic: 3.35 us -> 0 us
    pallas_call x0 -> x1, Pallas kernels: none -> 109 us  [shards(): pl.pallas_call(functools.partial(kernel, n_z, n_dp), out_shape=(act, act,...]
    all_gather x3 -> x0, blocking collectives: 83.2 us -> none  [the longest x1 28.7 us: shards(): lax.all_gather(hidden_share, 'expert', axis=0, tiled=True)]
    all_to_all x4 -> x0, starting transfers between devices: 63.1 us -> none  [the longest x1 24.2 us: shards(): lax.all_to_all(back_rows.reshape(experts, capacity, slices), 'dp', split_...]
    unnamed x1 -> x0, blocking collectives: 46 us -> none
    all_to_all x4 -> x0, waiting for transfers between devices: 32.8 us -> none  [the longest x1 12.1 us: shards(): lax.all_to_all(dbuf.reshape(experts, capacity, slices), 'dp', split_axis=...]
    unnamed x6 -> x0, starting transfers between devices: 14.9 us -> none
    dot_general x13 -> x0, matrix products: 13.9 us -> none  [the longest x1 1.76 us: shards(): jnp.dot(hidden, down_w, preferred_element_type=jnp.float32)]
    reshape x8 -> x0, local copies, waits for them, and re-layouts: 4.47 us -> none  [the longest x1 1.07 us: shards(): grad_back.reshape(experts * capacity, slices).astype(jnp.float32)]
  transfers between devices with their start and end apart: 10 -> 0, of which waited for: 3 -> 0; matrix products, arithmetic and copies ran while one was open for 6% -> 0% of each run, Pallas kernels for 0% -> 0%
where the time goes in v1:
time: 118 us
  Pallas kernels  109 us (92%)
  local copies, waits for them, and re-layouts  7.96 us (7%)
    pallas_call x1, Pallas kernels, shards(): pl.pallas_call(functools.partial(kernel, n_z, n_dp), out_shape=(act, act,...  109 us
    unnamed x15, local copies, waits for them, and re-layouts  7.96 us

profile of v1, /device:TPU:1, one launch (start us, length us, event | category | flops | bytes accessed | tf_op | source)
XLA Modules:
  0.0 117.6 jit_solution(7155599937321625923)
XLA Ops:
  0.6 0.0 copy-start.3
  0.6 1.4 %copy.12.ids_ref = s32[40,8]{1,0:T(8,128)} copy(s32[40,8]{0,1:T(8,128)} %param.8) | data formatting | bytes 2560 | tf_op args[1]
  2.0 0.0 copy-done.3
  2.0 0.7 copy.13.probs_ref
  2.7 109.0 %experts.1 = (bf16[40,256]{1,0:T(8,128)(2,1)}, bf16[40,256]{1,0:T(8,128)(2,1)}, bf16[1,1024,256]{2,1,0:T(8,128)(2,1)}, bf16[1,1024,256]{2,1,0:T(8,128)(2,1)}, bf16[1,1024,256]{2,1,0:T(8,128)(2,1)}) custom-call(s32[40,8]{1,0:T(8,128)} %copy.12.ids_ref, f32[40,8]{1,0:T(8,128)} %copy.13.probs_ref, bf16[40,256]{1,0:T(8,128)(2,1)} %tok_ref.1, ...), custom_call_target="tpu_custom_call" | custom-call | tf_op jit(solution)/shard_map/experts/pallas_call | solution.py:324
  111.7 0.0 copy-start.2
  111.7 1.3 %copy.19 = bf16[40,256]{1,0:T(8,128)(2,1)} copy(bf16[40,256]{1,0:T(8,128)(2,1)} %get-tuple-element.10) | data formatting | bytes 40960
  113.1 0.0 copy-done.2
  113.1 0.6 copy.20
  113.7 0.0 copy-start.1
  113.7 1.9 %copy.21 = bf16[1,1024,256]{2,1,0:T(8,128)(2,1)} copy(bf16[1,1024,256]{2,1,0:T(8,128)(2,1)} %get-tuple-element.12) | data formatting | bytes 1048576
  115.6 0.0 copy-done.1
  115.6 0.0 copy-start
  115.6 0.8 copy.22
  116.4 0.4 copy-done
  116.9 0.8 copy.23
Async XLA Ops:
  0.6 1.4 %copy-start.3 = (f32[40,8]{0,1:T(8,128)S(1)}, f32[40,8]{0,1:T(8,128)}, u32[]{:S(2)}) copy-start(f32[40,8]{0,1:T(8,128)} %param.9) | copy-start | bytes 3844
  111.7 1.4 %copy-start.2 = (bf16[40,256]{1,0:T(8,128)(2,1)S(1)}, bf16[40,256]{1,0:T(8,128)(2,1)}, u32[]{:S(2)}) copy-start(bf16[40,256]{1,0:T(8,128)(2,1)} %get-tuple-element.11) | copy-start | bytes 61444
  113.7 1.9 %copy-start.1 = (bf16[1,1024,256]{2,1,0:T(8,128)(2,1)S(1)}, bf16[1,1024,256]{2,1,0:T(8,128)(2,1)}, u32[]{:S(2)}) copy-start(bf16[1,1024,256]{2,1,0:T(8,128)(2,1)} %get-tuple-element.13) | copy-start | bytes 1572868
  115.6 1.2 %copy-start = (bf16[1,1024,256]{2,1,0:T(8,128)(2,1)S(1)}, bf16[1,1024,256]{2,1,0:T(8,128)(2,1)}, u32[]{:S(2)}) copy-start(bf16[1,1024,256]{2,1,0:T(8,128)(2,1)} %get-tuple-element.14) | copy-start | bytes 1572868

commit v2 on v1

--- a/solution.py
+++ b/solution.py
@@ -8,6 +8,8 @@
 from jax.sharding import PartitionSpec as P
 
 SLOTS = 8
+USED = 7
+CUTS = 4
 PAIR = 2 * SLOTS
 MESH = pl.DeviceIdType.MESH
 
@@ -25,16 +27,18 @@
 
 
 def kernel(
-    n_z, n_dp, ids_ref, probs_ref, tok_ref, cot_ref, gate_hbm, up_hbm, down_hbm,
-    mixed_ref, tgrad_ref, ggrad_hbm, ugrad_hbm, dgrad_hbm,
-    wts, grads, route, sbuf, inbuf, obuf, rbuf, xall, dall, part, landed, held,
-    w_sem, g_sem, in_send, in_recv, out_send, out_recv, rs_send, rs_recv, ag_send, ag_recv,
+    n_z, n_dp, ids_hbm, probs_hbm, tok_hbm, cot_hbm, gate_hbm, up_hbm, down_hbm,
+    route, rbuf, grads,
+    ids_ref, probs_ref, tok_ref, cot_ref, wts, sbuf, inbuf, obuf, xall, dall, pack, unpack, part, landed, held, hall,
+    w_sem, t_sem, in_send, in_recv, out_send, out_recv, rs_send, rs_recv, ag_send, ag_recv,
 ):
     cores, width, height, low, per = plan(n_z, n_dp)
     rows = per * SLOTS
     span = per * PAIR
-    half, cut = n_z // 2, rows // 2
-    n_tok, top = ids_ref.shape
+    quarter = wts.shape[1] // CUTS
+    packed = CUTS * per * USED
+    half, cut = n_z // 2, -(-packed // 32) * 16
+    top, n_tok = ids_ref.shape
     z = lax.axis_index("expert")
     g = lax.axis_index("dp")
     y, x, core = g // (width * cores), (g // cores) % width, g % cores
@@ -52,7 +56,13 @@
         pltpu.make_async_copy(src.at[0], wts.at[n], w_sem.at[n])
         for n, src in enumerate((gate_hbm, up_hbm, down_hbm))
     ]
-    for load in loads:
+    small = [
+        pltpu.make_async_copy(src, dst, t_sem.at[n])
+        for n, (src, dst) in enumerate(
+            ((ids_hbm, ids_ref), (probs_hbm, probs_ref), (tok_hbm, tok_ref), (cot_hbm, cot_ref))
+        )
+    ]
+    for load in small + loads:
         load.start()
 
     barrier = pltpu.get_barrier_semaphore()
@@ -70,7 +80,9 @@
     lx = (x + o_of % width) % width
     lc = (core + i_of % cores) % cores
     expert_of = (ly * width + lx) * cores + lc
-    ids, probs = ids_ref[...], probs_ref[...]
+    for load in small:
+        load.wait()
+    ids, probs = ids_ref[...].T, probs_ref[...].T
     named = jnp.zeros((n_tok, n_z * span), jnp.float32)
     weight = jnp.zeros((n_tok, n_z * span), jnp.float32)
     for k in range(top):
@@ -88,6 +100,16 @@
     high = scale.astype(jnp.bfloat16).astype(jnp.float32)
     mid = (scale - high).astype(jnp.bfloat16).astype(jnp.float32)
     route[...] = jnp.concatenate([plain, high, mid, scale - high - mid], axis=0).astype(jnp.bfloat16)
+
+    def place(dim, shape):
+        c = lax.broadcasted_iota(jnp.int32, shape, dim)
+        r, i, f = c % SLOTS, (c % rows) // SLOTS, c // rows
+        to = (f * per + i) * USED + r
+        return ((r < USED) & (to == lax.broadcasted_iota(jnp.int32, shape, 1 - dim))).astype(jnp.float32)
+
+    pack[...] = place(1, (packed, CUTS * rows)).astype(jnp.bfloat16)
+    unpack[...] = place(0, (CUTS * rows, packed)).astype(jnp.bfloat16)
+
     tok, cot = tok_ref[...].astype(jnp.float32), cot_ref[...].astype(jnp.float32)
     values = jnp.concatenate([tok, cot, cot, cot], axis=0).astype(jnp.bfloat16)
     sbuf[...] = matmul(route[...], values, (0, 0)).astype(jnp.bfloat16)
@@ -155,7 +177,11 @@
         for a, lhs in enumerate((xrows, xrows, drows)):
             product = matmul(lhs, wts[a], (1, 1)).astype(jnp.bfloat16)
             for n, o in enumerate(chunks):
-                part[a, o] = product[n * rows : (n + 1) * rows]
+                mine = product[n * rows : (n + 1) * rows]
+                stacked = jnp.concatenate(
+                    [mine[:, f * quarter : (f + 1) * quarter] for f in range(CUTS)], axis=0
+                )
+                part[a, o] = matmul(pack[...], stacked, (1, 0)).astype(jnp.bfloat16)
 
     sides = (z_right, z_left)
 
@@ -185,7 +211,7 @@
             device_id_type=MESH,
         )
 
-    halves = (pl.ds(0, cut), pl.ds(cut, cut))
+    halves = (pl.ds(0, cut), pl.ds(cut, packed - cut))
 
     partials([far])
     for a in range(3):
@@ -240,10 +266,16 @@
             ag_copy(d, 1, a, z).start()
 
     def outward(chunks):
-        lhs = [
-            jnp.concatenate([held[a, o] for o in chunks], axis=0) if len(chunks) > 1 else held[a, chunks[0]]
-            for a in range(3)
-        ]
+        lhs = []
+        for a in range(3):
+            whole = []
+            for o in chunks:
+                stacked = matmul(unpack[...], held[a, o], (1, 0)).astype(jnp.bfloat16)
+                whole.append(
+                    jnp.concatenate([stacked[f * rows : (f + 1) * rows] for f in range(CUTS)], axis=1)
+                )
+                hall[a, pl.ds(pl.multiple_of(o * rows, rows), rows), :] = whole[-1]
+            lhs.append(jnp.concatenate(whole, axis=0) if len(whole) > 1 else whole[0])
         back = matmul(lhs[0], wts[0], (1, 0)) + matmul(lhs[1], wts[1], (1, 0))
         out = matmul(lhs[2], wts[2], (1, 0))
         for n, o in enumerate(chunks):
@@ -276,21 +308,10 @@
             ag_copy(d, half, a, far, halves[d]).wait_recv()
     outward([far])
 
-    stores = []
-    for a, dst in enumerate((ggrad_hbm, ugrad_hbm, dgrad_hbm)):
-        whole = held[a].reshape(n_z * rows, -1)
-        rhs = (dall if a == 2 else xall)[...]
-        grads[a] = matmul(whole, rhs, (0, 0)).astype(jnp.bfloat16)
-        stores.append(pltpu.make_async_copy(grads.at[a], dst.at[0], g_sem.at[a]))
-        stores[-1].start()
+    for a in range(3):
+        grads[a] = matmul(hall[a], (dall if a == 2 else xall)[...], (0, 0)).astype(jnp.bfloat16)
 
     wait_rows(rbuf, 0, n_z * span, out_recv)
-    total = matmul(route[...], rbuf[...], (1, 0))
-    tgrad_ref[...] = total[:n_tok].astype(jnp.bfloat16)
-    mixed_ref[...] = (total[n_tok : 2 * n_tok] + total[2 * n_tok : 3 * n_tok] + total[3 * n_tok :]).astype(
-        jnp.bfloat16
-    )
-
     wait_rows(sbuf, 0, n_z * span - PAIR, in_send)
     wait_rows(obuf, 0, n_z * span - PAIR, out_send)
     for a in range(3):
@@ -305,6 +326,20 @@
                 rs_copy(d, s, a, z).wait_send()
                 ag_copy(d, s, a, z).wait_send()
 
+
+def finish(route, rbuf, grads, mixed_ref, tgrad_ref, ggrad_hbm, ugrad_hbm, dgrad_hbm, sem):
+    stores = [
+        pltpu.make_async_copy(grads.at[a], dst.at[0], sem.at[a])
+        for a, dst in enumerate((ggrad_hbm, ugrad_hbm, dgrad_hbm))
+    ]
+    for store in stores:
+        store.start()
+    n_tok = mixed_ref.shape[0]
+    total = matmul(route[...], rbuf[...], (1, 0))
+    tgrad_ref[...] = total[:n_tok].astype(jnp.bfloat16)
+    mixed_ref[...] = (total[n_tok : 2 * n_tok] + total[2 * n_tok : 3 * n_tok] + total[3 * n_tok :]).astype(
+        jnp.bfloat16
+    )
     for store in stores:
         store.wait()
 
@@ -314,33 +349,42 @@
     ff = w_gate.shape[1]
     rows = n_dp // n_z * SLOTS
     both = n_dp * PAIR
+    packed = CUTS * (n_dp // n_z) * USED
     half = n_z // 2
     bf16 = jnp.bfloat16
     vmem = pl.BlockSpec(memory_space=pltpu.VMEM)
-    anywhere = pl.BlockSpec(memory_space=pl.ANY)
+    anywhere = pl.BlockSpec(memory_space=pltpu.HBM)
     act = jax.ShapeDtypeStruct((n_tok, feats), bf16)
     grad = jax.ShapeDtypeStruct((1, ff, feats), bf16)
     dma = pltpu.SemaphoreType.DMA
-    return pl.pallas_call(
+    route, rbuf, grads = pl.pallas_call(
         functools.partial(kernel, n_z, n_dp),
-        out_shape=(act, act, grad, grad, grad),
-        in_specs=[vmem] * 4 + [anywhere] * 3,
-        out_specs=(vmem, vmem, anywhere, anywhere, anywhere),
-        scratch_shapes=[
-            pltpu.VMEM((3, ff, feats), bf16),
-            pltpu.VMEM((3, ff, feats), bf16),
+        out_shape=(
             pltpu.VMEM((4 * n_tok, both), bf16),
             pltpu.VMEM((both, feats), bf16),
+            pltpu.VMEM((3, ff, feats), bf16),
+        ),
+        in_specs=[anywhere] * 7,
+        out_specs=(vmem, vmem, vmem),
+        scratch_shapes=[
+            pltpu.VMEM(expert_ids.shape[::-1], jnp.int32),
+            pltpu.VMEM(expert_ids.shape[::-1], jnp.float32),
+            pltpu.VMEM((n_tok, feats), bf16),
+            pltpu.VMEM((n_tok, feats), bf16),
+            pltpu.VMEM((3, ff, feats), bf16),
             pltpu.VMEM((both, feats), bf16),
             pltpu.VMEM((both, feats), bf16),
             pltpu.VMEM((both, feats), bf16),
             pltpu.VMEM((n_z * rows, feats), bf16),
             pltpu.VMEM((n_z * rows, feats), bf16),
-            pltpu.VMEM((3, n_z, rows, ff), bf16),
-            pltpu.VMEM((2, half, 3, rows, ff), bf16),
-            pltpu.VMEM((3, n_z, rows, ff), bf16),
+            pltpu.VMEM((packed, CUTS * rows), bf16),
+            pltpu.VMEM((CUTS * rows, packed), bf16),
+            pltpu.VMEM((3, n_z, packed, ff // CUTS), bf16),
+            pltpu.VMEM((2, half, 3, packed, ff // CUTS), bf16),
+            pltpu.VMEM((3, n_z, packed, ff // CUTS), bf16),
+            pltpu.VMEM((3, n_z * rows, ff), bf16),
             dma((3,)),
-            dma((3,)),
+            dma((4,)),
             dma,
             dma((n_z,)),
             dma,
@@ -354,7 +398,16 @@
             collective_id=0, has_side_effects=True, vmem_limit_bytes=56 * 1024 * 1024
         ),
         name="experts",
-    )(expert_ids, gate_probs, tokens, cotangent, w_gate, w_up, w_down)
+    )(expert_ids.T, gate_probs.T, tokens, cotangent, w_gate, w_up, w_down)
+    return pl.pallas_call(
+        finish,
+        out_shape=(act, act, grad, grad, grad),
+        in_specs=[vmem] * 3,
+        out_specs=(vmem, vmem, anywhere, anywhere, anywhere),
+        scratch_shapes=[dma((3,))],
+        compiler_params=pltpu.CompilerParams(vmem_limit_bytes=16 * 1024 * 1024),
+        name="finish",
+    )(route, rbuf, grads)
 
 
 def solution(mesh):

time: 118 us -> 106 us (0.90)
  local copies, waits for them, and re-layouts: 7.96 us -> 0 us
  Pallas kernels: 109 us -> 105 us
    unnamed x15 -> x0, local copies, waits for them, and re-layouts: 7.96 us -> none
    pallas_call x1 -> x2, Pallas kernels: 109 us -> 105 us  [the longest x1 103 us: shards(): pl.pallas_call(functools.partial(kernel, n_z, n_dp), out_shape=(pltpu.VME...]
where the time goes in v2:
time: 106 us
  Pallas kernels  105 us (99%)
    pallas_call x1, Pallas kernels, shards(): pl.pallas_call(functools.partial(kernel, n_z, n_dp), out_shape=(pltpu.VME...  103 us

profile of v2, /device:TPU:1, one launch (start us, length us, event | category | flops | bytes accessed | tf_op | source)
XLA Modules:
  0.0 105.6 jit_solution(2495451085568534275)
XLA Ops:
  0.6 103.1 %experts.1 = (bf16[160,1024]{1,0:T(8,128)(2,1)S(1)}, bf16[1024,256]{1,0:T(8,128)(2,1)S(1)}, bf16[3,1024,256]{2,1,0:T(8,128)(2,1)S(1)}) custom-call(s32[8,40]{1,0:T(8,128)} %bitcast.2, f32[8,40]{1,0:T(8,128)} %bitcast.3, bf16[40,256]{1,0:T(8,128)(2,1)} %tok_hbm.1, bf16[40,256]{1,0:T(8,128)(2,1)} %cot_hbm.1, bf16[1,1024,256]{2,1,0:T(8,128)(2,1)} %gate_hbm.1, ...), custom_call_target="tpu_custom_call" | custom-call | tf_op jit(solution)/shard_map/experts/pallas_call | solution.py:360
  103.8 1.9 %finish.1 = (bf16[40,256]{1,0:T(8,128)(2,1)}, bf16[40,256]{1,0:T(8,128)(2,1)}, bf16[1,1024,256]{2,1,0:T(8,128)(2,1)}, bf16[1,1024,256]{2,1,0:T(8,128)(2,1)}, bf16[1,1024,256]{2,1,0:T(8,128)(2,1)}) custom-call(bf16[160,1024]{1,0:T(8,128)(2,1)S(1)} %get-tuple-element.8.route, bf16[1024,256]{1,0:T(8,128)(2,1)S(1)} %get-tuple-element.9.rbuf, ...), custom_call_target="tpu_custom_call" | custom-call | tf_op jit(solution)/shard_map/finish/pallas_call | solution.py:402

commit v3 on v2

--- a/solution.py
+++ b/solution.py
@@ -10,6 +10,7 @@
 SLOTS = 8
 USED = 7
 CUTS = 4
+PIECES = 5
 PAIR = 2 * SLOTS
 MESH = pl.DeviceIdType.MESH
 
@@ -37,19 +38,30 @@
     span = per * PAIR
     quarter = wts.shape[1] // CUTS
     packed = CUTS * per * USED
-    half, cut = n_z // 2, -(-packed // 32) * 16
+    half = n_z // 2
+    size = 3 * packed // PIECES // 16 * 16
+    starts = [m * size for m in range(PIECES)] + [3 * packed]
+    msgs = [(m, starts[m], starts[m + 1] - starts[m]) for m in range(PIECES)]
+    centre = PIECES // 2
+    split = size // 32 * 16
+    far_msgs = (
+        msgs[:centre] + [(centre, starts[centre], split)],
+        [(centre, starts[centre] + split, size - split)] + msgs[centre + 1 :],
+    )
+    rs_order = (msgs[centre + 1 :] + msgs[: centre + 1], msgs)
+    ag_order = (msgs, msgs[centre:] + msgs[:centre])
     top, n_tok = ids_ref.shape
     z = lax.axis_index("expert")
     g = lax.axis_index("dp")
     y, x, core = g // (width * cores), (g // cores) % width, g % cores
-    z_right, z_left = (z + 1) % n_z, (z + n_z - 1) % n_z
+    z_right, z_left = lax.rem(z + 1, n_z), lax.rem(z + n_z - 1, n_z)
 
     def partner(o, i, sign):
-        dy = o // width + low * (i // cores)
-        dx, dc = o % width, i % cores
-        py = (y + sign * dy + height) % height
-        px = (x + sign * dx + width) % width
-        pc = (core + sign * dc + cores) % cores
+        dy = lax.div(o, width) + low * (i // cores)
+        dx, dc = lax.rem(o, width), i % cores
+        py = lax.rem(y + sign * dy + height, height)
+        px = lax.rem(x + sign * dx + width, width)
+        pc = lax.rem(core + sign * dc + cores, cores)
         return (py * width + px) * cores + pc
 
     loads = [
@@ -69,7 +81,7 @@
 
     @pl.loop(1, n_dp)
     def _(step):
-        pl.semaphore_signal(barrier, inc=1, device_id={"dp": (g + step) % n_dp}, device_id_type=MESH)
+        pl.semaphore_signal(barrier, inc=1, device_id={"dp": lax.rem(g + step, n_dp)}, device_id_type=MESH)
 
     for near in (z_right, z_left):
         pl.semaphore_signal(barrier, inc=1, device_id={"expert": near}, device_id_type=MESH)
@@ -181,103 +193,116 @@
                 stacked = jnp.concatenate(
                     [mine[:, f * quarter : (f + 1) * quarter] for f in range(CUTS)], axis=0
                 )
-                part[a, o] = matmul(pack[...], stacked, (1, 0)).astype(jnp.bfloat16)
+                part[o, a * packed : (a + 1) * packed] = matmul(pack[...], stacked, (1, 0)).astype(jnp.bfloat16)
 
     sides = (z_right, z_left)
 
-    def rs_copy(d, s, a, o, at=None):
-        src, dst = part.at[a, o], landed.at[d, s, a]
-        if at is not None:
-            src, dst = src.at[at], dst.at[at]
+    def rs_copy(d, s, o, m, first, count):
+        at = pl.ds(first, count)
         return pltpu.make_async_remote_copy(
-            src_ref=src,
-            dst_ref=dst,
-            send_sem=rs_send.at[d, s, a],
-            recv_sem=rs_recv.at[d, s, a],
+            src_ref=part.at[o].at[at],
+            dst_ref=landed.at[d, s].at[at],
+            send_sem=rs_send.at[d, s, m],
+            recv_sem=rs_recv.at[d, s, m],
             device_id={"expert": sides[d]},
             device_id_type=MESH,
         )
 
-    def ag_copy(d, s, a, o, at=None):
-        src, dst = held.at[a, o], held.at[a, o]
-        if at is not None:
-            src, dst = src.at[at], dst.at[at]
+    def ag_copy(d, s, o, m, first, count):
+        at = pl.ds(first, count)
         return pltpu.make_async_remote_copy(
-            src_ref=src,
-            dst_ref=dst,
-            send_sem=ag_send.at[d, s, a],
-            recv_sem=ag_recv.at[d, s, a],
+            src_ref=held.at[o].at[at],
+            dst_ref=held.at[o].at[at],
+            send_sem=ag_send.at[d, s, m],
+            recv_sem=ag_recv.at[d, s, m],
             device_id={"expert": sides[d]},
             device_id_type=MESH,
         )
 
-    halves = (pl.ds(0, cut), pl.ds(cut, packed - cut))
-
     partials([far])
-    for a in range(3):
-        for d in range(2):
-            rs_copy(d, 0, a, far, halves[d]).start()
+    for n in range(centre + 1):
+        for d in range(2):
+            rs_copy(d, 0, far, *far_msgs[d][n]).start()
 
     def ends(s):
         return (z + half - s) % n_z, (z + half + s) % n_z
 
-    partials(ends(1))
-    for a in range(3):
-        for d in range(2):
-            o = ends(1)[d]
-            rs_copy(d, 0, a, o, halves[d]).wait_recv()
-            at = halves[d]
-            part[a, o, at, :] = (
-                part[a, o, at, :].astype(jnp.float32) + landed[d, 0, a, at, :].astype(jnp.float32)
-            ).astype(jnp.bfloat16)
-            rs_copy(d, 1, a, o).start()
+    def add_on(d, s, o, m, first, count):
+        rs_copy(d, s, o, m, first, count).wait_recv()
+        at = pl.ds(first, count)
+        part[o, at, :] = (
+            part[o, at, :].astype(jnp.float32) + landed[d, s, at, :].astype(jnp.float32)
+        ).astype(jnp.bfloat16)
+
+    near = ends(1)
+    partials(near)
+    for n in range(centre):
+        rs_copy(0, 1, near[0], *msgs[centre + 1 + n]).start()
+        rs_copy(1, 1, near[1], *msgs[n]).start()
+    for n in range(centre + 1):
+        for d in range(2):
+            add_on(d, 0, near[d], *far_msgs[d][n])
+            rs_copy(d, 1, near[d], *msgs[far_msgs[d][n][0]]).start()
 
     @pl.loop(2, half)
     def _(s):
         chunks = ends(s)
         partials(chunks)
-        for a in range(3):
+        for n in range(PIECES):
             for d in range(2):
-                o = chunks[d]
-                rs_copy(d, s - 1, a, o).wait_recv()
-                part[a, o] = (
-                    part[a, o].astype(jnp.float32) + landed[d, s - 1, a].astype(jnp.float32)
-                ).astype(jnp.bfloat16)
-                rs_copy(d, s, a, o).start()
+                add_on(d, s - 1, chunks[d], *rs_order[d][n])
+                rs_copy(d, s, chunks[d], *rs_order[d][n]).start()
 
     partials([z])
-    sums = []
-    for a in range(3):
-        for d in range(2):
-            rs_copy(d, half - 1, a, z).wait_recv()
-        sums.append(
-            part[a, z].astype(jnp.float32)
-            + landed[0, half - 1, a].astype(jnp.float32)
-            + landed[1, half - 1, a].astype(jnp.float32)
+
+    def landed_sum(a):
+        at = pl.ds(a * packed, packed)
+        return (
+            part[z, at, :].astype(jnp.float32)
+            + landed[0, half - 1, at, :].astype(jnp.float32)
+            + landed[1, half - 1, at, :].astype(jnp.float32)
         )
-    gate, up, hgrad = sums
+
+    def hold(a, value):
+        held[z, a * packed : (a + 1) * packed] = value.astype(jnp.bfloat16)
+
+    early = [msg for msg in msgs if msg[1] < 2 * packed]
+    late = [msg for msg in msgs if msg[1] >= 2 * packed]
+    ready = [msg for msg in msgs if msg[1] + msg[2] <= packed]
+    for msg in early:
+        for d in range(2):
+            rs_copy(d, half - 1, z, *msg).wait_recv()
+    gate, up = landed_sum(0), landed_sum(1)
     sig = jax.nn.sigmoid(gate)
     active = gate * sig
-    held[0, z] = (hgrad * up * sig * (1.0 + gate * (1.0 - sig))).astype(jnp.bfloat16)
-    held[1, z] = (hgrad * active).astype(jnp.bfloat16)
-    held[2, z] = (active * up).astype(jnp.bfloat16)
-    for a in range(3):
-        for d in range(2):
-            ag_copy(d, 1, a, z).start()
+    hold(0, active * up)
+    for msg in ready:
+        for d in range(2):
+            ag_copy(d, 1, z, *msg).start()
+    for msg in late:
+        for d in range(2):
+            rs_copy(d, half - 1, z, *msg).wait_recv()
+    hgrad = landed_sum(2)
+    hold(1, hgrad * active)
+    hold(2, hgrad * up * sig * (1.0 + gate * (1.0 - sig)))
+    for n in range(PIECES):
+        for d in range(2):
+            if ag_order[d][n] not in ready:
+                ag_copy(d, 1, z, *ag_order[d][n]).start()
 
     def outward(chunks):
         lhs = []
         for a in range(3):
             whole = []
             for o in chunks:
-                stacked = matmul(unpack[...], held[a, o], (1, 0)).astype(jnp.bfloat16)
+                stacked = matmul(unpack[...], held[o, a * packed : (a + 1) * packed], (1, 0)).astype(jnp.bfloat16)
                 whole.append(
                     jnp.concatenate([stacked[f * rows : (f + 1) * rows] for f in range(CUTS)], axis=1)
                 )
                 hall[a, pl.ds(pl.multiple_of(o * rows, rows), rows), :] = whole[-1]
             lhs.append(jnp.concatenate(whole, axis=0) if len(whole) > 1 else whole[0])
-        back = matmul(lhs[0], wts[0], (1, 0)) + matmul(lhs[1], wts[1], (1, 0))
-        out = matmul(lhs[2], wts[2], (1, 0))
+        out = matmul(lhs[0], wts[2], (1, 0))
+        back = matmul(lhs[1], wts[1], (1, 0)) + matmul(lhs[2], wts[0], (1, 0))
         for n, o in enumerate(chunks):
             mine = slice(n * rows, (n + 1) * rows)
             both = jnp.stack(
@@ -291,40 +316,42 @@
     @pl.loop(1, half - 1)
     def _(s):
         chunks = ((z - s + n_z) % n_z, (z + s) % n_z)
-        for a in range(3):
+        for n in range(PIECES):
             for d in range(2):
-                ag_copy(d, s, a, chunks[d]).wait_recv()
-                ag_copy(d, s + 1, a, chunks[d]).start()
+                ag_copy(d, s, chunks[d], *ag_order[d][n]).wait_recv()
+                ag_copy(d, s + 1, chunks[d], *ag_order[d][n]).start()
         outward(chunks)
 
     last = ((z - (half - 1) + n_z) % n_z, (z + half - 1) % n_z)
+    for n in range(PIECES):
+        for d in range(2):
+            ag_copy(d, half - 1, last[d], *ag_order[d][n]).wait_recv()
+            for part_msg in far_msgs[d]:
+                if part_msg[0] == ag_order[d][n][0]:
+                    ag_copy(d, half, last[d], *part_msg).start()
+    outward(last)
+    for d in range(2):
+        for msg in far_msgs[d]:
+            ag_copy(d, half, far, *msg).wait_recv()
+    outward([far])
+
     for a in range(3):
-        for d in range(2):
-            ag_copy(d, half - 1, a, last[d]).wait_recv()
-            ag_copy(d, half, a, last[d], halves[d]).start()
-    outward(last)
-    for a in range(3):
-        for d in range(2):
-            ag_copy(d, half, a, far, halves[d]).wait_recv()
-    outward([far])
-
-    for a in range(3):
-        grads[a] = matmul(hall[a], (dall if a == 2 else xall)[...], (0, 0)).astype(jnp.bfloat16)
+        grads[2 - a] = matmul(hall[a], (xall if a else dall)[...], (0, 0)).astype(jnp.bfloat16)
 
     wait_rows(rbuf, 0, n_z * span, out_recv)
     wait_rows(sbuf, 0, n_z * span - PAIR, in_send)
     wait_rows(obuf, 0, n_z * span - PAIR, out_send)
-    for a in range(3):
-        for d in range(2):
-            rs_copy(d, 0, a, far, halves[d]).wait_send()
-            ag_copy(d, half, a, far, halves[d]).wait_send()
+    for d in range(2):
+        for msg in far_msgs[d]:
+            rs_copy(d, 0, far, *msg).wait_send()
+            ag_copy(d, half, far, *msg).wait_send()
 
     @pl.loop(1, half)
     def _(s):
-        for a in range(3):
+        for msg in msgs:
             for d in range(2):
-                rs_copy(d, s, a, z).wait_send()
-                ag_copy(d, s, a, z).wait_send()
+                rs_copy(d, s, z, *msg).wait_send()
+                ag_copy(d, s, z, *msg).wait_send()
 
 
 def finish(route, rbuf, grads, mixed_ref, tgrad_ref, ggrad_hbm, ugrad_hbm, dgrad_hbm, sem):
@@ -379,9 +406,9 @@
             pltpu.VMEM((n_z * rows, feats), bf16),
             pltpu.VMEM((packed, CUTS * rows), bf16),
             pltpu.VMEM((CUTS * rows, packed), bf16),
-            pltpu.VMEM((3, n_z, packed, ff // CUTS), bf16),
-            pltpu.VMEM((2, half, 3, packed, ff // CUTS), bf16),
-            pltpu.VMEM((3, n_z, packed, ff // CUTS), bf16),
+            pltpu.VMEM((n_z, 3 * packed, ff // CUTS), bf16),
+            pltpu.VMEM((2, half, 3 * packed, ff // CUTS), bf16),
+            pltpu.VMEM((n_z, 3 * packed, ff // CUTS), bf16),
             pltpu.VMEM((3, n_z * rows, ff), bf16),
             dma((3,)),
             dma((4,)),
@@ -389,10 +416,10 @@
             dma((n_z,)),
             dma,
             dma,
-            dma((2, half, 3)),
-            dma((2, half, 3)),
-            dma((2, half + 1, 3)),
-            dma((2, half + 1, 3)),
+            dma((2, half, PIECES)),
+            dma((2, half, PIECES)),
+            dma((2, half + 1, PIECES)),
+            dma((2, half + 1, PIECES)),
         ],
         compiler_params=pltpu.CompilerParams(
             collective_id=0, has_side_effects=True, vmem_limit_bytes=56 * 1024 * 1024

time: 106 us -> 105 us (level)
  no operation moved by 1% of the time
where the time goes in v3:
time: 105 us
  Pallas kernels  104 us (99%)
    pallas_call x1, Pallas kernels, shards(): pl.pallas_call(functools.partial(kernel, n_z, n_dp), out_shape=(pltpu.VME...  102 us

profile of v3, /device:TPU:1, one launch (start us, length us, event | category | flops | bytes accessed | tf_op | source)
XLA Modules:
  0.0 104.6 jit_solution(10306833710902569273)
XLA Ops:
  0.6 102.1 %experts.1 = (bf16[160,1024]{1,0:T(8,128)(2,1)S(1)}, bf16[1024,256]{1,0:T(8,128)(2,1)S(1)}, bf16[3,1024,256]{2,1,0:T(8,128)(2,1)S(1)}) custom-call(s32[8,40]{1,0:T(8,128)} %bitcast.2, f32[8,40]{1,0:T(8,128)} %bitcast.3, bf16[40,256]{1,0:T(8,128)(2,1)} %tok_hbm.1, bf16[40,256]{1,0:T(8,128)(2,1)} %cot_hbm.1, bf16[1,1024,256]{2,1,0:T(8,128)(2,1)} %gate_hbm.1, ...), custom_call_target="tpu_custom_call" | custom-call | tf_op jit(solution)/shard_map/experts/pallas_call | solution.py:387
  102.8 1.9 %finish.1 = (bf16[40,256]{1,0:T(8,128)(2,1)}, bf16[40,256]{1,0:T(8,128)(2,1)}, bf16[1,1024,256]{2,1,0:T(8,128)(2,1)}, bf16[1,1024,256]{2,1,0:T(8,128)(2,1)}, bf16[1,1024,256]{2,1,0:T(8,128)(2,1)}) custom-call(bf16[160,1024]{1,0:T(8,128)(2,1)S(1)} %get-tuple-element.8.route, bf16[1024,256]{1,0:T(8,128)(2,1)S(1)} %get-tuple-element.9.rbuf, ...), custom_call_target="tpu_custom_call" | custom-call | tf_op jit(solution)/shard_map/finish/pallas_call | solution.py:429

commit v4 on v3

--- a/solution.py
+++ b/solution.py
@@ -173,7 +173,7 @@
     for load in loads:
         load.wait()
 
-    def partials(chunks):
+    def arrived(chunks):
         xs, ds = [], []
         for o in chunks:
             at = pl.multiple_of(o * span, span)
@@ -186,14 +186,21 @@
             dall[to, :] = ds[-1]
         xrows = jnp.concatenate(xs, axis=0) if len(xs) > 1 else xs[0]
         drows = jnp.concatenate(ds, axis=0) if len(ds) > 1 else ds[0]
-        for a, lhs in enumerate((xrows, xrows, drows)):
-            product = matmul(lhs, wts[a], (1, 1)).astype(jnp.bfloat16)
-            for n, o in enumerate(chunks):
-                mine = product[n * rows : (n + 1) * rows]
-                stacked = jnp.concatenate(
-                    [mine[:, f * quarter : (f + 1) * quarter] for f in range(CUTS)], axis=0
-                )
-                part[o, a * packed : (a + 1) * packed] = matmul(pack[...], stacked, (1, 0)).astype(jnp.bfloat16)
+        return xrows, xrows, drows
+
+    def partial(a, chunks, lhs):
+        product = matmul(lhs[a], wts[a], (1, 1)).astype(jnp.bfloat16)
+        for n, o in enumerate(chunks):
+            mine = product[n * rows : (n + 1) * rows]
+            stacked = jnp.concatenate(
+                [mine[:, f * quarter : (f + 1) * quarter] for f in range(CUTS)], axis=0
+            )
+            part[o, a * packed : (a + 1) * packed] = matmul(pack[...], stacked, (1, 0)).astype(jnp.bfloat16)
+
+    def partials(chunks):
+        lhs = arrived(chunks)
+        for a in range(3):
+            partial(a, chunks, lhs)
 
     sides = (z_right, z_left)
 
@@ -244,16 +251,27 @@
             add_on(d, 0, near[d], *far_msgs[d][n])
             rs_copy(d, 1, near[d], *msgs[far_msgs[d][n][0]]).start()
 
-    @pl.loop(2, half)
-    def _(s):
+    def rs_step(s, following):
         chunks = ends(s)
-        partials(chunks)
+        lhs = None
         for n in range(PIECES):
             for d in range(2):
                 add_on(d, s - 1, chunks[d], *rs_order[d][n])
                 rs_copy(d, s, chunks[d], *rs_order[d][n]).start()
-
-    partials([z])
+            lhs = arrived(following) if n == 0 else lhs
+            if n < 3:
+                partial(n, following, lhs)
+
+    if half > 2:
+        partials(ends(2))
+
+        @pl.loop(2, half - 1)
+        def _(s):
+            rs_step(s, ends(s + 1))
+
+        rs_step(half - 1, (z,))
+    else:
+        partials([z])
 
     def landed_sum(a):
         at = pl.ds(a * packed, packed)

time: 105 us -> 104 us (level)
  no operation moved by 1% of the time
where the time goes in v4:
time: 104 us
  Pallas kernels  104 us (100%)
    pallas_call x1, Pallas kernels, shards(): pl.pallas_call(functools.partial(kernel, n_z, n_dp), out_shape=(pltpu.VME...  102 us

profile of v4, /device:TPU:1, one launch (start us, length us, event | category | flops | bytes accessed | tf_op | source)
XLA Modules:
  0.0 104.3 jit_solution(12589408075694483947)
XLA Ops:
  0.6 101.8 %experts.1 = (bf16[160,1024]{1,0:T(8,128)(2,1)S(1)}, bf16[1024,256]{1,0:T(8,128)(2,1)S(1)}, bf16[3,1024,256]{2,1,0:T(8,128)(2,1)S(1)}) custom-call(s32[8,40]{1,0:T(8,128)} %bitcast.2, f32[8,40]{1,0:T(8,128)} %bitcast.3, bf16[40,256]{1,0:T(8,128)(2,1)} %tok_hbm.1, bf16[40,256]{1,0:T(8,128)(2,1)} %cot_hbm.1, bf16[1,1024,256]{2,1,0:T(8,128)(2,1)} %gate_hbm.1, ...), custom_call_target="tpu_custom_call" | custom-call | tf_op jit(solution)/shard_map/experts/pallas_call | solution.py:405
  102.4 1.8 %finish.1 = (bf16[40,256]{1,0:T(8,128)(2,1)}, bf16[40,256]{1,0:T(8,128)(2,1)}, bf16[1,1024,256]{2,1,0:T(8,128)(2,1)}, bf16[1,1024,256]{2,1,0:T(8,128)(2,1)}, bf16[1,1024,256]{2,1,0:T(8,128)(2,1)}) custom-call(bf16[160,1024]{1,0:T(8,128)(2,1)S(1)} %get-tuple-element.8.route, bf16[1024,256]{1,0:T(8,128)(2,1)S(1)} %get-tuple-element.9.rbuf, ...), custom_call_target="tpu_custom_call" | custom-call | tf_op jit(solution)/shard_map/finish/pallas_call | solution.py:447
